TPU v7x, 256 devices: a whole 4x4x8 slice. The times are simulated.
256 devices in a mesh: pa: 16 (over x, z_lo, core), pb: 16 (over y, z_hi).
Axes of the slice: x: 4, y: 4, z: 8 (z_hi: 4, z_lo: 2; z = z_hi * 2 + z_lo), core: 2. Of those that a mesh axis runs over, the one named last changes fastest.
Arguments:
- point_keys: bfloat16 [32768, 768], P(('pa', 'pb')), may hold values from -7 to 7
- point_values: bfloat16 [32768, 768], P(('pa', 'pb')), may hold values from -40 to 40
- out_grad: bfloat16 [32768, 768], P(('pa', 'pb')), may hold values from -512 to 512
- decoder_norm: float32 [12, 32768], P(None, ('pa', 'pb')), as said below
- latent_query: bfloat16 [1024, 768], P(('pa', 'pb')), may hold values from -4 to 4
- latent_out: bfloat16 [1024, 768], P(('pa', 'pb')), may hold values from -5 to 5
- encoder_norm: float32 [12, 1024], replicated, as said below
Outputs:
- keys_grad: bfloat16 [32768, 768], P(('pa', 'pb'))
- values_grad: bfloat16 [32768, 768], P(('pa', 'pb'))
- latent_grad: float32 [1024, 768], P(('pa', 'pb'))
Inputs may be any that keep to these rules, and one draw needn't show every extreme that they name: `decoder_norm`: each entry lies between log(1024) - 0.3 and log(1024) + 1.3. `encoder_norm`: each entry lies between log(32768) - 0.3 and log(32768) + 1.3.
All inputs are finite; a program needn't handle non-finite values.
Results may differ from a plain program's by a relative error of at most 0.004.
The roundings to bfloat16 on the way count: a program that leaves them out, or rounds other values in their place, can miss the bound.
Values may be sent and summed in bfloat16 or wider, within the bound.
A program may use at most 64 MiB of HBM per device.

v0:
```python
import jax
import jax.numpy as jnp
from jax import lax
from jax.sharding import PartitionSpec as P

HEADS = 12
HEAD_DIM = 64


def in_one_piece(arrays, axis, dim, along):
    widths = [a.shape[along] for a in arrays]
    both = jnp.concatenate(arrays, axis=along)
    result = lax.all_gather(both, axis, axis=dim, tiled=True)
    return tuple(jnp.split(result, [sum(widths[:k]) for k in range(1, len(widths))], axis=along))


def column(block, current):
    return lax.dynamic_slice_in_dim(block, current * HEAD_DIM, HEAD_DIM, 1)


def put_head(total, piece, current):
    return lax.dynamic_update_slice_in_dim(total, piece, current * HEAD_DIM, 1)


def add_head(total, piece, current):
    return put_head(total, column(total, current) + piece, current)


def across(left, right):
    return lax.dot_general(
        left, right, (((1,), (1,)), ((), ())), preferred_element_type=jnp.float32
    )


def down_rows(left, right):
    return lax.dot_general(
        left, right, (((0,), (0,)), ((), ())), preferred_element_type=jnp.float32
    )


def shards(
    point_keys, point_values, out_grad, decoder_norm, latent_query, latent_out, encoder_norm
):
    scale_factor = HEAD_DIM ** (-0.5)
    lat_all, out_all = in_one_piece((latent_query, latent_out), ("pa", "pb"), 0, 1)
    point_rows = point_keys.shape[0]
    latent_rows = lat_all.shape[0]
    width = point_keys.shape[1]

    def encoder_row(current):
        return lax.dynamic_slice_in_dim(encoder_norm, current, 1, 0)

    def pass_one(current, state):
        mix_acc, query_acc, key_acc, weighted_acc = state
        key_head = column(point_keys, current)
        grad_head = column(out_grad, current)
        lat_head = column(lat_all, current)
        scores = across(key_head, lat_head) * scale_factor
        decoder_weights = jnp.exp(scores - lax.dynamic_slice_in_dim(decoder_norm, current, 1, 0).T)
        decoder_gradient = across(grad_head, column(out_all, current))
        row_total = jnp.sum(decoder_weights * decoder_gradient, axis=1, keepdims=True)
        decoder_scores_grad = (decoder_weights * (decoder_gradient - row_total)).astype(
            jnp.bfloat16
        )
        mix_acc = put_head(
            mix_acc, down_rows(decoder_weights.astype(jnp.bfloat16), grad_head), current
        )
        query_acc = put_head(
            query_acc, down_rows(decoder_scores_grad, key_head) * scale_factor, current
        )
        key_acc = put_head(
            key_acc,
            jnp.dot(decoder_scores_grad, lat_head, preferred_element_type=jnp.float32)
            * scale_factor,
            current,
        )
        return (mix_acc, query_acc, key_acc, weighted_acc)

    weighted_blank = jnp.zeros((1, 1), jnp.float32)
    latent_blank = jnp.zeros((latent_rows, width), jnp.float32)
    begin = (
        latent_blank,
        latent_blank,
        jnp.zeros((point_rows, width), jnp.float32),
        weighted_blank,
    )
    mix_acc, query_acc, key_acc, weighted_acc = lax.fori_loop(0, HEADS, pass_one, begin)
    mix_grad = lax.psum(mix_acc, ("pa", "pb"))
    mixing_portion = mix_grad.astype(jnp.bfloat16)

    def pass_two(current, state):
        partial_rows, value_acc = state
        scores = across(column(point_keys, current), column(lat_all, current)) * scale_factor
        encoder_portion = jnp.exp(scores - encoder_row(current)).astype(jnp.bfloat16)
        mix_head = column(mixing_portion, current)
        encoder_gradient = across(column(point_values, current), mix_head)
        sums = jnp.sum(encoder_portion.astype(jnp.float32) * encoder_gradient, axis=0)[None, :]
        partial_rows = lax.dynamic_update_slice_in_dim(partial_rows, sums, current, 0)
        value_acc = put_head(
            value_acc,
            jnp.dot(encoder_portion, mix_head, preferred_element_type=jnp.float32),
            current,
        )
        return (partial_rows, value_acc)

    partial_rows, value_acc = lax.fori_loop(
        0,
        HEADS,
        pass_two,
        (jnp.zeros((HEADS, latent_rows), jnp.float32), jnp.zeros((point_rows, width), jnp.float32)),
    )
    column_total = lax.psum(partial_rows, ("pa", "pb"))

    def pass_three(current, state):
        query_acc, key_acc, value_acc = state
        key_head = column(point_keys, current)
        lat_head = column(lat_all, current)
        mix_head = column(mixing_portion, current)
        scores = across(key_head, lat_head) * scale_factor
        encoder = jnp.exp(scores - encoder_row(current))
        encoder_gradient = across(column(point_values, current), mix_head)
        encoder_scores_grad = (
            encoder * (encoder_gradient - lax.dynamic_slice_in_dim(column_total, current, 1, 0))
        ).astype(jnp.bfloat16)
        query_acc = add_head(
            query_acc, down_rows(encoder_scores_grad, key_head) * scale_factor, current
        )
        key_acc = add_head(
            key_acc,
            jnp.dot(encoder_scores_grad, lat_head, preferred_element_type=jnp.float32)
            * scale_factor,
            current,
        )
        return (query_acc, key_acc, value_acc)

    query_acc, key_acc, value_acc = lax.fori_loop(
        0, HEADS, pass_three, (query_acc, key_acc, value_acc)
    )
    latent_grad = lax.psum_scatter(query_acc, ("pa", "pb"), scatter_dimension=0, tiled=True)
    return (key_acc.astype(jnp.bfloat16), value_acc.astype(jnp.bfloat16), latent_grad)


def solution(mesh):
    in_specs = (
        P(("pa", "pb"), None),
        P(("pa", "pb"), None),
        P(("pa", "pb"), None),
        P(None, ("pa", "pb")),
        P(("pa", "pb"), None),
        P(("pa", "pb"), None),
        P(),
    )
    out_specs = (P(("pa", "pb"), None), P(("pa", "pb"), None), P(("pa", "pb"), None))
    return jax.shard_map(shards, mesh=mesh, in_specs=in_specs, out_specs=out_specs, check_vma=False)
```

profile of v0, /device:TPU:2, one launch (start us, length us, event | category | flops | bytes accessed | tf_op | source)
XLA Modules:
  0.0 1422.8 jit_solution(10542835375838273922)
XLA Ops:
  9.3 705.5 %all-gather.3.cloned.1.call-done = bf16[256,4,1536]{2,1,0:T(4,128)(2,1)} async-done(((bf16[1,4,1536]{2,1,0:T(4,128)(2,1)}), bf16[256,4,1536]{2,1,0:T(4,128)(2,1)}) %all-gather.3.cloned.1.call-update) | async-done | bytes 3145744 | tf_op jit(solution)/shard_map/all_gather | solution.py:13
  714.8 5.9 reshape.9
  720.7 2.1 fusion.49
  722.8 2.1 broadcast_in_dim.16
  724.9 2.1 broadcast_in_dim.16.clone
  727.0 84.2 %while.47 = (s32[]{:T(128)}, f32[1024,768]{0,1:T(8,128)}, f32[1024,768]{0,1:T(8,128)}, f32[128,768]{0,1:T(8,128)S(1)}, bf16[128,768]{1,0:T(8,128)(2,1)}, /*index...) while((s32[]{:T(128)}, f32[1024,768]{0,1:T(8,128)}, ...), condition=%wide.region_2.0_spmd, body=%wide.region_0.0_spmd.sunk | while | flops 85008256 | bytes 5414575 | solution.py:87
  811.1 3.6 copy.14
  814.7 131.6 %all-reduce.5 = bf16[1024,768]{1,0:T(8,128)(2,1)S(1)} all-reduce(f32[1024,768]{1,0:T(8,128)} %copy.14), channel_id=1, replica_groups=mesh['pa'=16,'pb'=16] {'pa','pb'}, use_global_device_ids=true, to_apply=%region_3.0 | all-reduce | flops 786432 | bytes 4718592 | tf_op jit(solution)/shard_map/psum | solution.py:88
  946.3 64.0 %while.48 = (s32[]{:T(128)}, f32[12,1024]{1,0:T(8,128)}, bf16[128,768]{0,1:T(8,128)(2,1)}, bf16[128,768]{1,0:T(8,128)(2,1)}, bf16[1024,768]{1,0:T(8,128)(2,1)S(1...) while((s32[]{:T(128)}, f32[12,1024]{1,0:T(8,128)}, ...), condition=%wide.region_6.0_spmd, body=%wide.region_4.0_spmd.sunk | while | flops 51117060 | bytes 1698987 | solution.py:106
  1010.3 74.3 %psum.15 = f32[12,1024]{1,0:T(8,128)} all-reduce(f32[12,1024]{1,0:T(8,128)} %get-tuple-element.457), channel_id=1, replica_groups=mesh['pa'=16,'pb'=16] {'pa','pb'}, use_global_device_ids=true, to_apply=%region_7.0 | all-reduce | flops 12288 | bytes 98304 | tf_op jit(solution)/shard_map/psum | solution.py:112
  1084.6 64.4 %while.49 = (s32[]{:T(128)}, f32[1024,768]{0,1:T(8,128)}, f32[128,768]{0,1:T(8,128)S(1)}, bf16[128,768]{1,0:T(8,128)(2,1)}, bf16[1024,768]{1,0:T(8,128)(2,1)S(1)...) while((s32[]{:T(128)}, f32[1024,768]{0,1:T(8,128)}, ...), condition=%wide.region_9.0_spmd, body=%wide.region_8.0_spmd.sunk | while | flops 67911680 | bytes 3338415 | solution.py:136
  1087.6 2.0 fusion.115
  1092.9 2.0 fusion.115
  1098.3 2.0 fusion.115
  1103.7 2.0 fusion.115
  1114.4 2.0 fusion.115
  1119.7 2.0 fusion.115
  1125.1 2.0 fusion.115
  1130.5 2.0 fusion.115
  1135.9 2.0 fusion.115
  1141.2 2.0 fusion.115
  1146.6 2.0 fusion.115
  1149.0 3.6 copy.17
  1154.3 260.3 %all-reduce.4.cloned.1.call-done = f32[1024,768]{1,0:T(8,128)} async-done(((f32[1024,768]{1,0:T(8,128)}), f32[1024,768]{1,0:T(8,128)}) %all-reduce.4.cloned.1.call-update) | async-done | bytes 3145744
  (206 shorter events, 194.6 us)
Async XLA Ops:
  7.2 707.6 %all-gather.3.cloned.1.call-start = ((), (), s32[]{:S(2)}) async-start(), calls=%async_computation | async-start | bytes 3158016 | tf_op jit(solution)/shard_map/all_gather | solution.py:13
  8.6 1406.0 %all-reduce.4.cloned.1.call-start = ((), (), s32[]{:S(2)}) async-start(), calls=%async_computation.1 | async-start | bytes 6291456
  1152.5 0.9 copy-start
Sparse Core Ops, SparseCore 0:
  10.4 704.3 all-gather.2
  1152.7 261.8 all-reduce.3
where the time goes:
time: 1430 us; the launch traced here: 1420 us
  waiting for transfers between devices  966 us (68%)
  blocking collectives  206 us (14%)
  matrix products  166 us (12%)
  local copies, waits for them, and re-layouts  66.2 us (5%)
    all_gather x1, waiting for transfers between devices, in_one_piece(): result = lax.all_gather(both, axis, axis=dim, tiled=True)  706 us
    unnamed x3, waiting for transfers between devices  260 us
    psum x1, blocking collectives, shards(): mix_grad = lax.psum(mix_acc, ('pa', 'pb'))  132 us
    dot_general x72, matrix products, across(): lax.dot_general(left, right, (((1,), (1,)), ((), ())), preferred_element_...  79.1 us
    psum x1, blocking collectives, shards(): column_total = lax.psum(partial_rows, ('pa', 'pb'))  74.3 us
    dot_general x36, matrix products, down_rows(): lax.dot_general(left, right, (((0,), (0,)), ((), ())), preferred_element_...  66.2 us
  transfers between devices with their start and end apart: 2, of which 2 were waited for; matrix products, arithmetic and copies ran while one was open for 0% of the time, Pallas kernels for 0%

commit v1 on v0

--- a/solution.py
+++ b/solution.py
@@ -1,3 +1,4 @@
+import functools
 import jax
 import jax.numpy as jnp
 from jax import lax
@@ -5,6 +6,13 @@
 
 HEADS = 12
 HEAD_DIM = 64
+
+
+def time_the_quotas(array_here, device_axis):
+    return jnp.sum(jax.lax.all_gather(array_here, device_axis), axis=0)
+
+
+try_all_surface = functools.partial(time_the_quotas, device_axis=("pa", "pb"))
 
 
 def in_one_piece(arrays, axis, dim, along):
@@ -109,7 +117,7 @@
         pass_two,
         (jnp.zeros((HEADS, latent_rows), jnp.float32), jnp.zeros((point_rows, width), jnp.float32)),
     )
-    column_total = lax.psum(partial_rows, ("pa", "pb"))
+    column_total = try_all_surface(partial_rows)
 
     def pass_three(current, state):
         query_acc, key_acc, value_acc = state

time: 1430 us -> 2100 us (1.47)
  waiting for transfers between devices: 966 us -> 1700 us
  blocking collectives: 206 us -> 132 us
    all_gather x0 -> x1, waiting for transfers between devices: none -> 727 us  [time_the_quotas(): return jnp.sum(jax.lax.all_gather(array_here, device_axis), axis=0)]
    psum x1 -> x0, blocking collectives: 74.3 us -> none  [shards(): column_total = lax.psum(partial_rows, ('pa', 'pb'))]
    unnamed x3 -> x4, waiting for transfers between devices: 260 us -> 264 us
  transfers between devices with their start and end apart: 2 -> 3, of which waited for: 2 -> 3; matrix products, arithmetic and copies ran while one was open for 0% -> 0% of each run, Pallas kernels for 0% -> 0%
where the time goes in v1:
time: 2100 us; the launch traced here: 2090 us
  waiting for transfers between devices  1700 us (81%)
  matrix products  169 us (8%)
  blocking collectives  132 us (6%)
  local copies, waits for them, and re-layouts  68 us (3%)
    all_gather x1, waiting for transfers between devices, time_the_quotas(): return jnp.sum(jax.lax.all_gather(array_here, device_axis), axis=0)  727 us
    all_gather x1, waiting for transfers between devices, in_one_piece(): result = lax.all_gather(both, axis, axis=dim, tiled=True)  706 us
    unnamed x4, waiting for transfers between devices  264 us
    psum x1, blocking collectives, shards(): mix_grad = lax.psum(mix_acc, ('pa', 'pb'))  132 us
    dot_general x72, matrix products, across(): lax.dot_general(left, right, (((1,), (1,)), ((), ())), preferred_element_...  81.6 us
    dot_general x36, matrix products, down_rows(): lax.dot_general(left, right, (((0,), (0,)), ((), ())), preferred_element_...  66.2 us
  transfers between devices with their start and end apart: 3, of which 3 were waited for; matrix products, arithmetic and copies ran while one was open for 0% of the time, Pallas kernels for 0%

profile of v1, /device:TPU:2, one launch (start us, length us, event | category | flops | bytes accessed | tf_op | source)
XLA Modules:
  0.0 2090.5 jit_solution(11692065867671285971)
XLA Ops:
  9.3 705.5 %all-gather.6.cloned.1.call-done = bf16[256,4,1536]{2,1,0:T(4,128)(2,1)} async-done(((bf16[1,4,1536]{2,1,0:T(4,128)(2,1)}), bf16[256,4,1536]{2,1,0:T(4,128)(2,1)}) %all-gather.6.cloned.1.call-update) | async-done | bytes 3145744 | tf_op jit(solution)/shard_map/all_gather | solution.py:21
  714.8 5.9 reshape.10
  720.7 3.2 fusion.49
  723.9 2.0 broadcast_in_dim.16
  726.0 2.0 broadcast_in_dim.16.clone
  728.1 86.7 %while.47 = (s32[]{:T(128)}, f32[1024,768]{0,1:T(8,128)}, f32[1024,768]{0,1:T(8,128)}, f32[128,768]{0,1:T(8,128)S(1)}, bf16[128,768]{1,0:T(8,128)(2,1)}, /*index...) while((s32[]{:T(128)}, f32[1024,768]{0,1:T(8,128)}, ...), condition=%wide.region_2.0_spmd, body=%wide.region_0.0_spmd.sunk | while | flops 85008256 | bytes 5414575 | solution.py:95
  814.7 3.6 copy.14
  818.3 131.5 %all-reduce.5 = bf16[1024,768]{1,0:T(8,128)(2,1)S(1)} all-reduce(f32[1024,768]{1,0:T(8,128)} %copy.14), channel_id=1, replica_groups=mesh['pa'=16,'pb'=16] {'pa','pb'}, use_global_device_ids=true, to_apply=%region_3.0 | all-reduce | flops 786432 | bytes 4718592 | tf_op jit(solution)/shard_map/psum | solution.py:96
  949.8 64.0 %while.48 = (s32[]{:T(128)}, f32[12,1024]{1,0:T(8,128)}, bf16[128,768]{0,1:T(8,128)(2,1)}, bf16[128,768]{1,0:T(8,128)(2,1)}, bf16[1024,768]{1,0:T(8,128)(2,1)S(1...) while((s32[]{:T(128)}, f32[12,1024]{1,0:T(8,128)}, ...), condition=%wide.region_6.0_spmd, body=%wide.region_4.0_spmd.sunk | while | flops 51117060 | bytes 1698987 | solution.py:114
  1013.9 726.6 %all-gather.8.cloned.1.call-done = f32[256,12,1024]{2,1,0:T(8,128)} async-done(((f32[1,12,1024]{2,1,0:T(8,128)}), f32[256,12,1024]{2,1,0:T(8,128)}) %all-gather.8.cloned.1.call-update) | async-done | bytes 12582928 | tf_op jit(solution)/shard_map/all_gather | solution.py:12
  1740.5 7.3 reduce_sum.35
  1747.9 64.4 %while.49 = (s32[]{:T(128)}, f32[1024,768]{0,1:T(8,128)}, f32[128,768]{0,1:T(8,128)S(1)}, bf16[128,768]{1,0:T(8,128)(2,1)}, bf16[1024,768]{1,0:T(8,128)(2,1)S(1)...) while((s32[]{:T(128)}, f32[1024,768]{0,1:T(8,128)}, ...), condition=%wide.region_9.0_spmd, body=%wide.region_8.0_spmd.sunk | while | flops 67911680 | bytes 3338415 | solution.py:144
  1750.9 2.0 fusion.115
  1766.9 2.0 fusion.115
  1772.3 2.0 fusion.115
  1777.7 2.0 fusion.115
  1783.1 2.0 fusion.115
  1788.4 2.0 fusion.115
  1793.8 2.0 fusion.115
  1799.2 2.0 fusion.115
  1804.5 2.0 fusion.115
  1809.9 2.0 fusion.115
  1812.3 3.5 copy.17
  1818.4 264.2 %all-reduce.4.cloned.1.call-done = f32[1024,768]{1,0:T(8,128)} async-done(((f32[1024,768]{1,0:T(8,128)}), f32[1024,768]{1,0:T(8,128)}) %all-reduce.4.cloned.1.call-update) | async-done | bytes 3145744
  (209 shorter events, 200.0 us)
Async XLA Ops:
  7.2 707.6 %all-gather.6.cloned.1.call-start = ((), (), s32[]{:S(2)}) async-start(), calls=%async_computation | async-start | bytes 3158016 | tf_op jit(solution)/shard_map/all_gather | solution.py:21
  8.6 1732.0 %all-gather.8.cloned.1.call-start = ((), (), s32[]{:S(2)}) async-start(), calls=%async_computation.1 | async-start | bytes 16842752 | tf_op jit(solution)/shard_map/all_gather | solution.py:12
  1013.9 1068.8 %all-reduce.4.cloned.1.call-start = ((), (), s32[]{:S(2)}) async-start(), calls=%async_computation.2 | async-start | bytes 6291456
  1815.9 0.9 copy-start
Sparse Core Ops, SparseCore 0:
  10.4 704.3 all-gather.5
  1014.0 726.5 all-gather.7
  1816.0 266.5 all-reduce.3
